TPU v7x, 32 devices: a whole 2x2x4 slice. The times are simulated.
32 devices in a mesh: grp: 2 (over y), row: 4 (over z), col: 2 (over x), rep: 2 (over core).
Axes of the slice: x: 2, y: 2, z: 4, core: 2. Of those that a mesh axis runs over, the one named last changes fastest.
Arguments:
- f_rta: float32 [3, 8, 20480], P(None, None, ('grp', 'row', 'col', 'rep')), parts along dimension 2, may hold values from -6 to 6
- relax_time: float32 [8, 20480], P(None, ('grp', 'row', 'col', 'rep')), parts along dimension 1, may hold values from 0.15 to 1.2
- scatter_tiles: bfloat16 [4096, 128, 128], P(('grp', 'row', 'col', 'rep')), parts along dimension 0, may hold values from -0.109375 to 0.109375
- tile_row: int32 [4096], P(('grp', 'row', 'col', 'rep')), parts along dimension 0, may hold values from 0 to 19
- tile_col: int32 [4096], P(('grp', 'row', 'col', 'rep')), parts along dimension 0, may hold values from 0 to 79, as said below
Outputs:
- f_out: float32 [3, 8, 20480], P(None, None, ('grp', 'row', 'col', 'rep')), parts along dimension 2
There are 2 independent parts, one for each index of `grp`. A program takes and returns all parts, laid end to end along the dimension named above; each array names one. Nothing has to cross between parts.
Inputs may be any that keep to these rules, and one draw needn't show every extreme that they name: `tile_col`: A tile held by the device at col index c has a column block b owned by that col index: (b // 10) % 2 == c. Block b lives on the device at row index b // 20, col index (b // 10) % 2, rep index (b // 5) % 2. Tiles may repeat a block pair; their terms add.
All inputs are finite; a program needn't handle non-finite values.
Results may differ from a plain program's by a relative error of at most 0.0021.
Values may be sent and summed in bfloat16 or wider, within the bound.
A program may use at most 64 MiB of HBM per device.

v0:
```python
import jax
import jax.numpy as jnp
from jax import lax
from jax.sharding import PartitionSpec as P

DIRS = 3
TEMPS = 8
TILE = 128
BLK_DEV = 5
ITERS = 2


def shards(f_rta, relax_time, scatter_tiles, tile_row, tile_col):
    components = DIRS * TEMPS
    shard_width = f_rta.shape[-1]
    col_count = lax.axis_size("col")
    rep_count = lax.axis_size("rep")
    group_size = BLK_DEV * rep_count
    group_rows = group_size * col_count
    slab_index = tile_col // (group_size * col_count) * group_size + tile_col % group_size
    local_rows = jnp.arange(group_rows, dtype=jnp.int32)
    onehot = (local_rows[:, None] == tile_row[None, :]).astype(jnp.float32)
    current = f_rta
    for sweep in range(ITERS):
        vector_bf = current.astype(jnp.bfloat16).reshape(components, shard_width)
        column_slab = lax.all_gather(vector_bf, ("row", "rep"), axis=1, tiled=True)
        slab_blocks = column_slab.reshape(components, -1, TILE)
        picked = jnp.take(slab_blocks, slab_index, axis=1)
        products = jnp.einsum(
            "krc,dkc->kdr", scatter_tiles, picked, preferred_element_type=jnp.float32
        )
        block_sums = jnp.einsum("gk,kdr->dgr", onehot, products, precision=lax.Precision.HIGHEST)
        summed = lax.psum_scatter(
            block_sums.reshape(components, group_rows * TILE),
            ("col", "rep"),
            scatter_dimension=1,
            tiled=True,
        )
        current = f_rta + relax_time[None] * summed.reshape(DIRS, TEMPS, shard_width)
    return current


def solution(mesh):
    in_specs = (
        P(None, None, ("grp", "row", "col", "rep")),
        P(None, ("grp", "row", "col", "rep")),
        P(("grp", "row", "col", "rep"), None, None),
        P(("grp", "row", "col", "rep")),
        P(("grp", "row", "col", "rep")),
    )
    out_specs = P(None, None, ("grp", "row", "col", "rep"))
    return jax.shard_map(shards, mesh=mesh, in_specs=in_specs, out_specs=out_specs, check_vma=False)
```

profile of v0, /device:TPU:0, one launch (start us, length us, event | category | flops | bytes accessed | tf_op | source)
XLA Modules:
  0.0 102.3 jit_solution(230761099990534125)
XLA Ops:
  6.5 0.7 compare_and_fusion
  7.2 0.8 convert_bitcast_fusion
  8.1 15.9 %all_gather.6 = bf16[24,5120]{1,0:T(8,128)(2,1)S(1)} all-gather(bf16[24,640]{1,0:T(8,128)(2,1)S(1)} %convert_bitcast_fusion), channel_id=1, replica_groups=mesh['grp'=2,'row'=4,'col'=2,'rep'=2] {'row','rep'}, dimensions={1}, use_global_device_ids=true | all-gather | bytes 276480 | tf_op jit(solution)/shard_map/all_gather | solution.py:26
  24.0 0.8 gather_fusion
  24.7 0.0 copy-start.2
  24.7 4.5 %fusion.6 = f32[128,24,128]{2,1,0:T(8,128)S(1)} fusion(bf16[128,128,128]{2,1,0:T(8,128)(2,1)} %param.9, bf16[128,24,128]{2,1,0:T(8,128)(2,1)S(1)} %gather_fusion, pred[128]{0:T(512)(128)(4,1)S(1)} %get-tuple-element.6), kind=kOutput, calls=%fused_computation.8 | convolution fusion | flops 101056512 | bytes 6553728 | tf_op jit(solution)/shard_map/krc,dkc->kdr/dot_general | solution.py:29
  29.2 0.0 copy-done.2
  29.2 0.0 copy-start
  29.3 0.0 copy-start.1
  29.3 0.7 fusion.2
  30.0 0.7 copy.23
  30.8 0.0 reduce-scatter.3.cloned.1.call-update
  30.8 0.0 reduce-scatter.5.cloned.1.call-start
  30.8 21.1 %reduce-scatter.3.cloned.1.call-done = f32[24,640]{1,0:T(8,128)} async-done(((f32[24,2560]{1,0:T(8,128)}), f32[24,640]{1,0:T(8,128)}) %reduce-scatter.3.cloned.1.call-update) | async-done | bytes 61456 | tf_op jit(solution)/shard_map/reduce_scatter | solution.py:33
  52.0 0.0 copy-done.1
  52.0 0.8 fusion.17
  52.8 14.3 %all_gather.7 = bf16[24,5120]{1,0:T(8,128)(2,1)S(1)} all-gather(bf16[24,640]{1,0:T(8,128)(2,1)S(1)} %fusion.17), channel_id=1, replica_groups=mesh['grp'=2,'row'=4,'col'=2,'rep'=2] {'row','rep'}, dimensions={1}, use_global_device_ids=true | all-gather | bytes 276480 | tf_op jit(solution)/shard_map/all_gather | solution.py:26
  67.1 0.8 gather_fusion.1
  67.9 4.5 %fusion.4 = f32[128,24,128]{2,1,0:T(8,128)S(1)} fusion(bf16[128,128,128]{2,1,0:T(8,128)(2,1)} %param.9, bf16[128,24,128]{2,1,0:T(8,128)(2,1)S(1)} %gather_fusion.1, pred[128]{0:T(512)(128)(4,1)S(1)} %get-tuple-element.6), kind=kOutput, calls=%fused_computation.6 | convolution fusion | flops 101056512 | bytes 6553728 | tf_op jit(solution)/shard_map/krc,dkc->kdr/dot_general | solution.py:29
  72.4 0.8 fusion
  73.1 0.7 copy.22
  73.9 0.0 reduce-scatter.5.cloned.1.call-update
  73.9 20.1 %reduce-scatter.5.cloned.1.call-done = f32[24,640]{1,0:T(8,128)} async-done(((f32[24,2560]{1,0:T(8,128)}), f32[24,640]{1,0:T(8,128)}) %reduce-scatter.5.cloned.1.call-update) | async-done | bytes 61456 | tf_op jit(solution)/shard_map/reduce_scatter | solution.py:33
  94.0 1.5 %fusion.14 = f32[3,8,640]{2,1,0:T(8,128)} fusion(f32[3,8,640]{2,1,0:T(8,128)S(1)} %copy-done, f32[24,640]{1,0:T(8,128)} %reduce-scatter.5.cloned.1.call-done, f32[8,640]{1,0:T(8,128)S(1)} %copy-done.1), kind=kLoop, calls=%fused_computation.21 | loop fusion | flops 30720 | bytes 204800 | tf_op jit(solution)/shard_map/add | solution.py:39
  (5 shorter events, 0.1 us)
Async XLA Ops:
  6.5 45.4 %reduce-scatter.3.cloned.1.call-start = ((), (), s32[]{:S(2)}) async-start(), calls=%async_computation.2 | async-start | bytes 307200 | tf_op jit(solution)/shard_map/reduce_scatter | solution.py:33
  24.7 4.5 %copy-start.2 = (s32[128]{0:T(128)S(1)}, s32[128]{0:T(128)}, u32[]{:S(2)}) copy-start(s32[128]{0:T(128)} %param.10) | copy-start | bytes 1540
  29.2 22.7 %copy-start = (f32[3,8,640]{2,1,0:T(8,128)S(1)}, f32[3,8,640]{2,1,0:T(8,128)}, u32[]{:S(2)}) copy-start(f32[3,8,640]{2,1,0:T(8,128)} %param.7) | copy-start | bytes 184324
  29.3 22.7 %copy-start.1 = (f32[8,640]{1,0:T(8,128)S(1)}, f32[8,640]{1,0:T(8,128)}, u32[]{:S(2)}) copy-start(f32[8,640]{1,0:T(8,128)} %param.8) | copy-start | bytes 61444
  30.8 63.2 %reduce-scatter.5.cloned.1.call-start = ((), (), s32[]{:S(2)}) async-start(), calls=%async_computation.3 | async-start | bytes 307200 | tf_op jit(solution)/shard_map/reduce_scatter | solution.py:33
Sparse Core Ops, SparseCore 0:
  30.9 21.0 reduce-scatter.2
  74.0 19.9 reduce-scatter.4
where the time goes:
time: 103 us; the launch traced here: 102 us
  waiting for transfers between devices  41.3 us (40%)
  blocking collectives  30.1 us (29%)
  between operations  13.5 us (13%)
  matrix products  10.5 us (10%)
  other arithmetic  3.82 us (4%)
  local copies, waits for them, and re-layouts  3.09 us (3%)
    reduce_scatter x2, waiting for transfers between devices, shards(): lax.psum_scatter(block_sums.reshape(components, group_rows * TILE), ('col...  41.2 us
    all_gather x2, blocking collectives, shards(): column_slab = lax.all_gather(vector_bf, ('row', 'rep'), axis=1, tiled=True)  30.1 us
    dot_general x2, matrix products, shards(): jnp.einsum('krc,dkc->kdr', scatter_tiles, picked, preferred_element_type=...  8.99 us
  transfers between devices with their start and end apart: 2, of which 2 were waited for; matrix products, arithmetic and copies ran while one was open for 0% of the time, Pallas kernels for 0%

commit v1 on v0

v1 whole, which is shorter than its diff:
```python
import functools

import jax
import jax.numpy as jnp
from jax import lax
from jax.experimental import pallas as pl
from jax.experimental.pallas import tpu as pltpu
from jax.sharding import PartitionSpec as P

DIRS = 3
TEMPS = 8
COMP = DIRS * TEMPS
TILE = 128
BLK_DEV = 5
ITERS = 2
UNROLL = 16
CHUNKS = 4
ROWS = BLK_DEV * COMP
PAD = 128
MESH = pl.DeviceIdType.MESH


def kernel(sizes, f_ref, relax_ref, row_ref, col_ref, tiles_hbm, out_ref,
           tiles, vsend, slab, vec, chain, part, recv, table_v, table,
           tile_sem, table_sem, vs_send, vs_recv, fw_send, fw_recv, p_send, p_recv):
    n_row, n_col, n_rep, n_tiles = sizes
    grp, row = lax.axis_index("grp"), lax.axis_index("row")
    col, rep = lax.axis_index("col"), lax.axis_index("rep")
    per = n_tiles // CHUNKS

    row_peers = list(range(1, n_row))
    sum_peers = [(dc, dr) for dc in range(n_col) for dr in range(n_rep) if (dc, dr) != (0, 0)]
    rep_peers = list(range(1, n_rep))

    def at_row(step):
        return (grp, lax.rem(row + step, n_row), col, rep)

    def at_sum(dc, dr):
        return (grp, row, lax.rem(col + dc, n_col), lax.rem(rep + dr, n_rep))

    barrier = pltpu.get_barrier_semaphore()
    for step in row_peers:
        pl.semaphore_signal(barrier, inc=1, device_id=at_row(step), device_id_type=MESH)
    for dc, dr in sum_peers:
        pl.semaphore_signal(barrier, inc=1, device_id=at_sum(dc, dr), device_id_type=MESH)

    loads = []
    for i in range(CHUNKS):
        load = pltpu.make_async_copy(tiles_hbm.at[pl.ds(i * per, per)], tiles.at[pl.ds(i * per, per)], tile_sem.at[i])
        load.start()
        loads.append(load)

    def pack(it, source):
        blocks = [source[:, b * TILE:(b + 1) * TILE] for b in range(BLK_DEV)]
        blocks.append(jnp.zeros((PAD - ROWS, TILE), jnp.float32))
        vsend[it] = jnp.concatenate(blocks, axis=0).astype(jnp.bfloat16)

    pack(0, f_ref[...])
    pl.semaphore_wait(barrier, len(row_peers) + len(sum_peers))

    def gather_start(it):
        own = row * n_rep + rep
        sends = []
        for step in row_peers:
            copy = pltpu.make_async_remote_copy(
                src_ref=vsend.at[it], dst_ref=slab.at[it, own],
                send_sem=vs_send.at[it, step], recv_sem=vs_recv.at[it, step],
                device_id=at_row(step), device_id_type=MESH)
            copy.start()
            sends.append(copy)
        for step in rep_peers:
            copy = pltpu.make_async_remote_copy(
                src_ref=vsend.at[it], dst_ref=slab.at[it, own],
                send_sem=fw_send.at[it, 0, step], recv_sem=fw_recv.at[it, 0, step],
                device_id=at_sum(0, step), device_id_type=MESH)
            copy.start()
            sends.append(copy)
        return sends

    def unpack(it, index, value):
        vec[pl.ds(index * BLK_DEV, BLK_DEV)] = (
            value.astype(jnp.float32)[:ROWS].reshape(BLK_DEV, COMP, TILE))

    def gather_finish(it, sends):
        unpack(it, row * n_rep + rep, vsend[it])
        forwards = []
        for step in row_peers:
            origin = lax.rem(row + n_row - step, n_row)
            slot = origin * n_rep + rep
            pltpu.make_async_remote_copy(
                src_ref=vsend.at[it], dst_ref=slab.at[it, slot],
                send_sem=vs_send.at[it, step], recv_sem=vs_recv.at[it, step],
                device_id=at_row(step), device_id_type=MESH).wait_recv()
            for other in rep_peers:
                copy = pltpu.make_async_remote_copy(
                    src_ref=slab.at[it, slot], dst_ref=slab.at[it, slot],
                    send_sem=fw_send.at[it, step, other], recv_sem=fw_recv.at[it, step, other],
                    device_id=at_sum(0, other), device_id_type=MESH)
                copy.start()
                forwards.append(copy)
            unpack(it, slot, slab[it, slot])
        for step in [0] + row_peers:
            origin = lax.rem(row + n_row - step, n_row)
            for other in rep_peers:
                slot = origin * n_rep + lax.rem(rep + n_rep - other, n_rep)
                pltpu.make_async_remote_copy(
                    src_ref=vsend.at[it], dst_ref=slab.at[it, slot],
                    send_sem=fw_send.at[it, step, other], recv_sem=fw_recv.at[it, step, other],
                    device_id=at_sum(0, other), device_id_type=MESH).wait_recv()
                unpack(it, slot, slab[it, slot])
        return sends + forwards

    pending = gather_start(0)

    rows_lane = jnp.broadcast_to(row_ref[...], (n_tiles, n_tiles))
    rows_sub = rows_lane.T
    sub = lax.broadcasted_iota(jnp.int32, (n_tiles, n_tiles), 0)
    lane = lax.broadcasted_iota(jnp.int32, (n_tiles, n_tiles), 1)
    before = (rows_sub == rows_lane) & (sub < lane)
    previous = jnp.max(jnp.where(before, sub + 1, 0), axis=0, keepdims=True)
    last = jnp.max(jnp.where(rows_sub == lane, sub + 1, 0), axis=0, keepdims=True)
    group_size = BLK_DEV * n_rep
    span = group_size * n_col
    magic = -(-65536 // span)
    assert (magic * span - 65536) * span * n_row < 65536
    columns = col_ref[...]
    quotient = (columns * magic) >> 16
    rest = columns - quotient * span
    for _ in range(n_col - 1):
        rest = jnp.where(rest >= group_size, rest - group_size, rest)
    block = quotient * group_size + rest
    table_v[0:1, :] = previous
    table_v[1:2, :] = last
    table_v[2:3, :] = block
    table_copy = pltpu.make_async_copy(table_v, table, table_sem)
    table_copy.start()
    chain[0] = jnp.zeros((COMP, TILE), jnp.float32)
    table_copy.wait()

    def multiply(first, count):
        def body(i, carry):
            base = first + i * UNROLL
            products = []
            for u in range(UNROLL):
                picked = vec[table[2, base + u]].astype(jnp.bfloat16)
                products.append(lax.dot_general(
                    picked, tiles[base + u], (((1,), (1,)), ((), ())),
                    preferred_element_type=jnp.float32))
            for u in range(UNROLL):
                chain[base + u + 1] = chain[table[0, base + u]] + products[u]
            return carry
        lax.fori_loop(0, count // UNROLL, body, 0)

    for it in range(ITERS):
        pending = gather_finish(it, pending)
        if it == 0:
            for i in range(CHUNKS):
                loads[i].wait()
                multiply(i * per, per)
        else:
            multiply(0, n_tiles)

        for dc, dr in reversed(sum_peers):
            owner = lax.rem(col + dc, n_col) * n_rep + lax.rem(rep + dr, n_rep)
            index = dc * n_rep + dr
            for b in range(BLK_DEV):
                part[it, index, b] = chain[table[1, owner * BLK_DEV + b]]
            copy = pltpu.make_async_remote_copy(
                src_ref=part.at[it, index], dst_ref=recv.at[it, index],
                send_sem=p_send.at[it, index], recv_sem=p_recv.at[it, index],
                device_id=at_sum(dc, dr), device_id_type=MESH)
            copy.start()
            pending.append(copy)
        owner = col * n_rep + rep
        sums = [chain[table[1, owner * BLK_DEV + b]] for b in range(BLK_DEV)]
        for dc, dr in sum_peers:
            index = dc * n_rep + dr
            pltpu.make_async_remote_copy(
                src_ref=part.at[it, index], dst_ref=recv.at[it, index],
                send_sem=p_send.at[it, index], recv_sem=p_recv.at[it, index],
                device_id=at_sum(dc, dr), device_id_type=MESH).wait_recv()
            sums = [sums[b] + recv[it, index, b] for b in range(BLK_DEV)]
        summed = jnp.concatenate(sums, axis=1)
        relax = jnp.concatenate([relax_ref[...]] * DIRS, axis=0)
        current = f_ref[...] + relax * summed
        if it + 1 < ITERS:
            pack(it + 1, current)
            pending = pending + gather_start(it + 1)
        else:
            out_ref[...] = current
    for copy in pending:
        copy.wait_send()


def shards(sizes, f_rta, relax_time, scatter_tiles, tile_row, tile_col):
    n_row, n_col, n_rep, n_tiles = sizes
    width = f_rta.shape[-1]
    members, slots = n_col * n_rep, n_row * n_rep
    dma = pltpu.SemaphoreType.DMA
    vmem = pl.BlockSpec(memory_space=pltpu.VMEM)
    out = pl.pallas_call(
        functools.partial(kernel, sizes),
        out_shape=jax.ShapeDtypeStruct((COMP, width), jnp.float32),
        in_specs=[vmem, vmem, vmem, vmem, pl.BlockSpec(memory_space=pl.ANY)],
        out_specs=vmem,
        scratch_shapes=[
            pltpu.VMEM((n_tiles, TILE, TILE), jnp.bfloat16),
            pltpu.VMEM((ITERS, PAD, TILE), jnp.bfloat16),
            pltpu.VMEM((ITERS, slots, PAD, TILE), jnp.bfloat16),
            pltpu.VMEM((slots * BLK_DEV, COMP, TILE), jnp.float32),
            pltpu.VMEM((n_tiles + 1, COMP, TILE), jnp.float32),
            pltpu.VMEM((ITERS, members, BLK_DEV, COMP, TILE), jnp.float32),
            pltpu.VMEM((ITERS, members, BLK_DEV, COMP, TILE), jnp.float32),
            pltpu.VMEM((8, n_tiles), jnp.int32),
            pltpu.SMEM((8, n_tiles), jnp.int32),
            dma((CHUNKS,)),
            dma,
            dma((ITERS, n_row)),
            dma((ITERS, n_row)),
            dma((ITERS, n_row, n_rep)),
            dma((ITERS, n_row, n_rep)),
            dma((ITERS, members)),
            dma((ITERS, members)),
        ],
        compiler_params=pltpu.CompilerParams(
            collective_id=0, has_side_effects=True, vmem_limit_bytes=40 * 2**20),
    )(
        f_rta.reshape(COMP, width),
        relax_time,
        tile_row.reshape(1, n_tiles),
        tile_col.reshape(1, n_tiles),
        scatter_tiles,
    )
    return out.reshape(DIRS, TEMPS, width)


def solution(mesh):
    in_specs = (
        P(None, None, ("grp", "row", "col", "rep")),
        P(None, ("grp", "row", "col", "rep")),
        P(("grp", "row", "col", "rep"), None, None),
        P(("grp", "row", "col", "rep")),
        P(("grp", "row", "col", "rep")),
    )
    out_specs = P(None, None, ("grp", "row", "col", "rep"))

    def whole(f_rta, relax_time, scatter_tiles, tile_row, tile_col):
        n_tiles = tile_row.shape[0] // mesh.size
        sizes = (mesh.shape["row"], mesh.shape["col"], mesh.shape["rep"], n_tiles)
        return jax.shard_map(
            functools.partial(shards, sizes), mesh=mesh, in_specs=in_specs,
            out_specs=out_specs, check_vma=False,
        )(f_rta, relax_time, scatter_tiles, tile_row, tile_col)

    return whole
```

time: 103 us -> 36.3 us (0.35)
  waiting for transfers between devices: 41.3 us -> 0 us
  Pallas kernels: 0 us -> 30.4 us
  blocking collectives: 30.1 us -> 0 us
  between operations: 13.5 us -> 0.01 us
  matrix products: 10.5 us -> 0 us
  other arithmetic: 3.82 us -> 0 us
  local copies, waits for them, and re-layouts: 3.09 us -> 5.68 us
    reduce_scatter x2 -> x0, waiting for transfers between devices: 41.2 us -> none  [shards(): lax.psum_scatter(block_sums.reshape(components, group_rows * TILE), ('col...]
    pallas_call x0 -> x1, Pallas kernels: none -> 30.4 us  [shards(): pl.pallas_call(functools.partial(kernel, sizes), out_shape=jax.ShapeDtype...]
    all_gather x2 -> x0, blocking collectives: 30.1 us -> none  [shards(): column_slab = lax.all_gather(vector_bf, ('row', 'rep'), axis=1, tiled=True)]
    dot_general x4 -> x0, matrix products: 10.5 us -> none  [the longest x2 8.99 us: shards(): jnp.einsum('krc,dkc->kdr', scatter_tiles, picked, preferred_element_type=...]
    unnamed x8 -> x11, local copies, waits for them, and re-layouts: 1.51 us -> 5.68 us
    reshape x2 -> x0, other arithmetic: 1.68 us -> none  [shards(): vector_bf = current.astype(jnp.bfloat16).reshape(components, shard_width)]
    gather x2 -> x0, local copies, waits for them, and re-layouts: 1.5 us -> none  [shards(): picked = jnp.take(slab_blocks, slab_index, axis=1)]
    add x1 -> x0, other arithmetic: 1.46 us -> none  [shards(): f_rta + relax_time[None] * summed.reshape(DIRS, TEMPS, shard_width)]
  transfers between devices with their start and end apart: 2 -> 0, of which waited for: 2 -> 0; matrix products, arithmetic and copies ran while one was open for 0% -> 0% of each run, Pallas kernels for 0% -> 0%
where the time goes in v1:
time: 36.3 us; the launch traced here: 36.1 us
  Pallas kernels  30.4 us (84%)
  local copies, waits for them, and re-layouts  5.68 us (16%)
    pallas_call x1, Pallas kernels, shards(): pl.pallas_call(functools.partial(kernel, sizes), out_shape=jax.ShapeDtype...  30.4 us
    unnamed x11, local copies, waits for them, and re-layouts  5.68 us

profile of v1, /device:TPU:0, one launch (start us, length us, event | category | flops | bytes accessed | tf_op | source)
XLA Modules:
  0.0 36.1 jit_solution(16895436935517845942)
XLA Ops:
  0.0 0.0 copy-start
  0.0 2.2 %copy-done = bf16[128,128,128]{2,1,0:T(8,128)(2,1)S(1)} copy-done((bf16[128,128,128]{2,1,0:T(8,128)(2,1)S(1)}, bf16[128,128,128]{2,1,0:T(8,128)(2,1)}, u32[]{:S(2)}) %copy-start) | copy-done | bytes 4194328
  2.2 0.0 copy-start.1
  2.2 0.8 %copy-done.1 = f32[3,8,640]{2,1,0:T(8,128)S(1)} copy-done((f32[3,8,640]{2,1,0:T(8,128)S(1)}, f32[3,8,640]{2,1,0:T(8,128)}, u32[]{:S(2)}) %copy-start.1) | copy-done | bytes 61464
  3.0 0.0 copy-start.2
  3.0 0.7 %copy-done.2 = f32[8,640]{1,0:T(8,128)S(1)} copy-done((f32[8,640]{1,0:T(8,128)S(1)}, f32[8,640]{1,0:T(8,128)}, u32[]{:S(2)}) %copy-start.2) | copy-done | bytes 20504
  3.7 0.0 copy-start.3
  3.7 0.7 %copy-done.3 = s32[128]{0:T(128)S(1)} copy-done((s32[128]{0:T(128)S(1)}, s32[128]{0:T(128)}, u32[]{:S(2)}) %copy-start.3) | copy-done | bytes 536
  4.4 0.0 copy-start.4
  4.4 0.7 %copy-done.4 = s32[128]{0:T(128)S(1)} copy-done((s32[128]{0:T(128)S(1)}, s32[128]{0:T(128)}, u32[]{:S(2)}) %copy-start.4) | copy-done | bytes 536
  5.1 30.4 %shard_map.55 = f32[24,640]{1,0:T(8,128)S(1)} custom-call(f32[24,640]{1,0:T(8,128)S(1)} %bitcast.5, f32[8,640]{1,0:T(8,128)S(1)} %copy-done.2, s32[1,128]{1,0:T(1,128)S(1)} %bitcast.6, s32[1,128]{1,0:T(1,128)S(1)} %bitcast.7, bf16[128,128,128]{2,1,0:T(8,128)(2,1)S(1)} %copy-done), custom_call_target="tpu_custom_call" | custom-call | tf_op jit(solution)/shard_map/pallas_call | solution.py:201
  35.4 0.6 %copy.7 = f32[3,8,640]{2,1,0:T(8,128)} copy(f32[3,8,640]{2,1,0:T(8,128)S(1)} %bitcast.4) | data formatting | bytes 122880
Async XLA Ops:
  0.0 2.2 %copy-start = (bf16[128,128,128]{2,1,0:T(8,128)(2,1)S(1)}, bf16[128,128,128]{2,1,0:T(8,128)(2,1)}, u32[]{:S(2)}) copy-start(bf16[128,128,128]{2,1,0:T(8,128)(2,1)} %tiles_hbm.1) | copy-start | bytes 12582916
  2.2 0.8 %copy-start.1 = (f32[3,8,640]{2,1,0:T(8,128)S(1)}, f32[3,8,640]{2,1,0:T(8,128)}, u32[]{:S(2)}) copy-start(f32[3,8,640]{2,1,0:T(8,128)} %param.5) | copy-start | bytes 184324
  3.0 0.7 %copy-start.2 = (f32[8,640]{1,0:T(8,128)S(1)}, f32[8,640]{1,0:T(8,128)}, u32[]{:S(2)}) copy-start(f32[8,640]{1,0:T(8,128)} %relax_ref.1) | copy-start | bytes 61444
  3.7 0.7 %copy-start.3 = (s32[128]{0:T(128)S(1)}, s32[128]{0:T(128)}, u32[]{:S(2)}) copy-start(s32[128]{0:T(128)} %param.8) | copy-start | bytes 1540
  4.4 0.7 %copy-start.4 = (s32[128]{0:T(128)S(1)}, s32[128]{0:T(128)}, u32[]{:S(2)}) copy-start(s32[128]{0:T(128)} %param.9) | copy-start | bytes 1540

commit v2 on v1

--- a/solution.py
+++ b/solution.py
@@ -13,16 +13,15 @@
 TILE = 128
 BLK_DEV = 5
 ITERS = 2
-UNROLL = 16
 CHUNKS = 4
 ROWS = BLK_DEV * COMP
 PAD = 128
 MESH = pl.DeviceIdType.MESH
 
 
-def kernel(sizes, f_ref, relax_ref, row_ref, col_ref, tiles_hbm, out_ref,
-           tiles, vsend, slab, vec, chain, part, recv, table_v, table,
-           tile_sem, table_sem, vs_send, vs_recv, fw_send, fw_recv, p_send, p_recv):
+def kernel(sizes, f_hbm, relax_hbm, row_hbm, col_hbm, tiles_hbm, out_ref,
+           f_ref, relax_ref, row_ref, col_ref, tiles, turned, vsend, slab, vec, chain, part, recv, table_v, table,
+           tile_sem, in_sem, table_sem, vs_send, vs_recv, fw_send, fw_recv, p_send, p_recv):
     n_row, n_col, n_rep, n_tiles = sizes
     grp, row = lax.axis_index("grp"), lax.axis_index("row")
     col, rep = lax.axis_index("col"), lax.axis_index("rep")
@@ -31,6 +30,8 @@
     row_peers = list(range(1, n_row))
     sum_peers = [(dc, dr) for dc in range(n_col) for dr in range(n_rep) if (dc, dr) != (0, 0)]
     rep_peers = list(range(1, n_rep))
+
+    wait_order = sorted(row_peers, key=lambda step: (min(step, n_row - step), step))
 
     def at_row(step):
         return (grp, lax.rem(row + step, n_row), col, rep)
@@ -44,6 +45,12 @@
     for dc, dr in sum_peers:
         pl.semaphore_signal(barrier, inc=1, device_id=at_sum(dc, dr), device_id_type=MESH)
 
+    small = []
+    for i, (source, target) in enumerate(
+            [(f_hbm, f_ref), (row_hbm, row_ref), (col_hbm, col_ref), (relax_hbm, relax_ref)]):
+        load = pltpu.make_async_copy(source, target, in_sem.at[i])
+        load.start()
+        small.append(load)
     loads = []
     for i in range(CHUNKS):
         load = pltpu.make_async_copy(tiles_hbm.at[pl.ds(i * per, per)], tiles.at[pl.ds(i * per, per)], tile_sem.at[i])
@@ -55,13 +62,14 @@
         blocks.append(jnp.zeros((PAD - ROWS, TILE), jnp.float32))
         vsend[it] = jnp.concatenate(blocks, axis=0).astype(jnp.bfloat16)
 
+    small[0].wait()
     pack(0, f_ref[...])
     pl.semaphore_wait(barrier, len(row_peers) + len(sum_peers))
 
     def gather_start(it):
         own = row * n_rep + rep
         sends = []
-        for step in row_peers:
+        for step in wait_order:
             copy = pltpu.make_async_remote_copy(
                 src_ref=vsend.at[it], dst_ref=slab.at[it, own],
                 send_sem=vs_send.at[it, step], recv_sem=vs_recv.at[it, step],
@@ -84,7 +92,7 @@
     def gather_finish(it, sends):
         unpack(it, row * n_rep + rep, vsend[it])
         forwards = []
-        for step in row_peers:
+        for step in wait_order:
             origin = lax.rem(row + n_row - step, n_row)
             slot = origin * n_rep + rep
             pltpu.make_async_remote_copy(
@@ -98,8 +106,10 @@
                     device_id=at_sum(0, other), device_id_type=MESH)
                 copy.start()
                 forwards.append(copy)
+        for step in wait_order:
+            slot = lax.rem(row + n_row - step, n_row) * n_rep + rep
             unpack(it, slot, slab[it, slot])
-        for step in [0] + row_peers:
+        for step in [0] + wait_order:
             origin = lax.rem(row + n_row - step, n_row)
             for other in rep_peers:
                 slot = origin * n_rep + lax.rem(rep + n_rep - other, n_rep)
@@ -112,6 +122,8 @@
 
     pending = gather_start(0)
 
+    for load in small[1:]:
+        load.wait()
     rows_lane = jnp.broadcast_to(row_ref[...], (n_tiles, n_tiles))
     rows_sub = rows_lane.T
     sub = lax.broadcasted_iota(jnp.int32, (n_tiles, n_tiles), 0)
@@ -135,30 +147,21 @@
     table_copy = pltpu.make_async_copy(table_v, table, table_sem)
     table_copy.start()
     chain[0] = jnp.zeros((COMP, TILE), jnp.float32)
+    for i in range(CHUNKS):
+        loads[i].wait()
+        for k in range(i * per, (i + 1) * per):
+            turned[k] = tiles[k].T
     table_copy.wait()
 
-    def multiply(first, count):
-        def body(i, carry):
-            base = first + i * UNROLL
-            products = []
-            for u in range(UNROLL):
-                picked = vec[table[2, base + u]].astype(jnp.bfloat16)
-                products.append(lax.dot_general(
-                    picked, tiles[base + u], (((1,), (1,)), ((), ())),
-                    preferred_element_type=jnp.float32))
-            for u in range(UNROLL):
-                chain[base + u + 1] = chain[table[0, base + u]] + products[u]
-            return carry
-        lax.fori_loop(0, count // UNROLL, body, 0)
+    def multiply():
+        for k in range(n_tiles):
+            picked = vec[table[2, k]].astype(jnp.bfloat16)
+            product = jnp.dot(picked, turned[k], preferred_element_type=jnp.float32)
+            chain[k + 1] = chain[table[0, k]] + product
 
     for it in range(ITERS):
         pending = gather_finish(it, pending)
-        if it == 0:
-            for i in range(CHUNKS):
-                loads[i].wait()
-                multiply(i * per, per)
-        else:
-            multiply(0, n_tiles)
+        multiply()
 
         for dc, dr in reversed(sum_peers):
             owner = lax.rem(col + dc, n_col) * n_rep + lax.rem(rep + dr, n_rep)
@@ -201,9 +204,14 @@
     out = pl.pallas_call(
         functools.partial(kernel, sizes),
         out_shape=jax.ShapeDtypeStruct((COMP, width), jnp.float32),
-        in_specs=[vmem, vmem, vmem, vmem, pl.BlockSpec(memory_space=pl.ANY)],
+        in_specs=[pl.BlockSpec(memory_space=pltpu.HBM)] * 5,
         out_specs=vmem,
         scratch_shapes=[
+            pltpu.VMEM((COMP, width), jnp.float32),
+            pltpu.VMEM((TEMPS, width), jnp.float32),
+            pltpu.VMEM((1, n_tiles), jnp.int32),
+            pltpu.VMEM((1, n_tiles), jnp.int32),
+            pltpu.VMEM((n_tiles, TILE, TILE), jnp.bfloat16),
             pltpu.VMEM((n_tiles, TILE, TILE), jnp.bfloat16),
             pltpu.VMEM((ITERS, PAD, TILE), jnp.bfloat16),
             pltpu.VMEM((ITERS, slots, PAD, TILE), jnp.bfloat16),
@@ -214,6 +222,7 @@
             pltpu.VMEM((8, n_tiles), jnp.int32),
             pltpu.SMEM((8, n_tiles), jnp.int32),
             dma((CHUNKS,)),
+            dma((4,)),
             dma,
             dma((ITERS, n_row)),
             dma((ITERS, n_row)),
@@ -223,7 +232,7 @@
             dma((ITERS, members)),
         ],
         compiler_params=pltpu.CompilerParams(
-            collective_id=0, has_side_effects=True, vmem_limit_bytes=40 * 2**20),
+            collective_id=0, has_side_effects=True, vmem_limit_bytes=56 * 2**20),
     )(
         f_rta.reshape(COMP, width),
         relax_time,

time: 36.3 us -> 28.7 us (0.79)
  local copies, waits for them, and re-layouts: 5.68 us -> 1.46 us
  Pallas kernels: 30.4 us -> 27.1 us
    unnamed x11 -> x1, local copies, waits for them, and re-layouts: 5.68 us -> 1.46 us
    pallas_call x1, Pallas kernels: 30.4 us -> 27.1 us  [shards(): pl.pallas_call(functools.partial(kernel, sizes), out_shape=jax.ShapeDtype...]
where the time goes in v2:
time: 28.7 us; the launch traced here: 28.6 us
  Pallas kernels  27.1 us (94%)
  local copies, waits for them, and re-layouts  1.46 us (5%)
    pallas_call x1, Pallas kernels, shards(): pl.pallas_call(functools.partial(kernel, sizes), out_shape=jax.ShapeDtype...  27.1 us
    unnamed x1, local copies, waits for them, and re-layouts  1.46 us

profile of v2, /device:TPU:0, one launch (start us, length us, event | category | flops | bytes accessed | tf_op | source)
XLA Modules:
  0.0 28.6 jit_solution(15239186625092031560)
XLA Ops:
  0.0 27.1 %shard_map.55 = f32[24,640]{1,0:T(8,128)} custom-call(f32[24,640]{1,0:T(8,128)} %bitcast.5, f32[8,640]{1,0:T(8,128)} %relax_hbm.1, s32[1,128]{1,0:T(1,128)} %bitcast.6, s32[1,128]{1,0:T(1,128)} %bitcast.7, bf16[128,128,128]{2,1,0:T(8,128)(2,1)} %tiles_hbm.1), custom_call_target="tpu_custom_call" | custom-call | tf_op jit(solution)/shard_map/pallas_call | solution.py:204
  27.2 1.5 %copy.7 = f32[3,8,640]{2,1,0:T(8,128)} copy(f32[3,8,640]{2,1,0:T(8,128)} %bitcast.4) | data formatting | bytes 122880
